TPU v7x, 32 devices: a whole 2x2x4 slice. The times are simulated.
32 devices in a mesh: dp: 2 (over y), expert: 16 (over z, x, core).
Axes of the slice: x: 2, y: 2, z: 4, core: 2. Of those that a mesh axis runs over, the one named last changes fastest.
Arguments:
- cache: bfloat16 [4, 64, 1152], P('dp'), may hold values from -6 to 6
- requests: int32 [2, 16, 2], P(None, 'expert'), may hold values from 0 to 3
- routes: int32 [4096, 1], P('expert'), may hold values from 0 to 15; in each aligned block of 256 rows (0 to 255, 256 to 511, ...) at most 20 rows name the same one
- combine_weight: float32 [4096, 1], P('expert'), may hold values from 0.2 to 1
- proj_weight: bfloat16 [1152, 2048], P('expert', 'dp'), may hold values from -1 to 1
- norm_gain: float32 [2048], replicated, may hold values from 0.5 to 1.5
- gate_weight: bfloat16 [16, 2048, 1408], P('expert', None, 'dp'), may hold values from -0.125 to 0.125
- up_weight: bfloat16 [16, 2048, 1408], P('expert', None, 'dp'), may hold values from -0.125 to 0.125
- down_weight: bfloat16 [16, 1408, 2048], P('expert', None, 'dp'), may hold values from -0.15625 to 0.15625
- cotangent: bfloat16 [4096, 2048], P('expert', 'dp'), may hold values from -6 to 6
Outputs:
- mixed: bfloat16 [4096, 2048], P('expert', 'dp')
- down_grad: bfloat16 [16, 1408, 2048], P('expert', None, 'dp')
Inputs may be any that keep to these rules, and one draw needn't show every extreme that they name: `routes`: among the 256 tokens of one column no expert is named more than 20 times, and in every draw some column names some expert exactly 20 times.
All inputs are finite; a program needn't handle non-finite values.
Results may differ from a plain program's by a relative error of at most 0.012.
Values may be sent and summed in bfloat16 or wider, within the bound.
A program may use at most 64 MiB of HBM per device.

v0:
```python
import jax
import jax.numpy as jnp
from jax import lax
from jax.sharding import PartitionSpec as P

BF = jnp.bfloat16
F32 = jnp.float32


def dot(a, b, dims=((1,), (0,))):
    return lax.dot_general(a, b, (dims, ((), ())), preferred_element_type=F32)


def body(
    cache,
    requests,
    routes,
    combine_weight,
    proj_weight,
    norm_gain,
    gate_weight,
    up_weight,
    down_weight,
    cotangent,
):
    width = cotangent.shape[1]
    n_expert = lax.axis_size("expert")
    experts = n_expert * gate_weight.shape[0]
    block, feat = cache.shape[1:]
    feats = lax.all_gather(cache, "dp", axis=0, tiled=True).reshape(-1, feat)
    lanes = width // n_expert
    piece = lax.all_to_all(
        proj_weight.reshape(-1, n_expert, lanes), "expert", split_axis=1, concat_axis=0, tiled=True
    ).reshape(feat, lanes)
    part = dot(feats, piece).astype(BF)
    projected = lax.all_gather(part, ("dp", "expert"), axis=1, tiled=True)
    values = projected.astype(F32)
    mean_square = jnp.mean(values * values, axis=1)
    table = (values * lax.rsqrt(mean_square + 1e-06)[:, None] * norm_gain[None, :]).astype(BF)
    table_rows = table.shape[0]
    token_row = (
        requests.reshape(-1)[:, None] * block + jnp.arange(block, dtype=jnp.int32)[None, :]
    ).reshape(-1)
    tokens = token_row.shape[0]
    capacity = max(2, 5 * tokens // (4 * experts))
    expert_id = routes[:, 0]
    order = jnp.arange(tokens, dtype=jnp.int32)
    earlier = (expert_id[:, None] == expert_id[None, :]) & (order[None, :] < order[:, None])
    slot_rank = jnp.sum(earlier.astype(jnp.int32), axis=1)
    position = expert_id * capacity + slot_rank
    hit = jnp.arange(experts * capacity, dtype=jnp.int32)[:, None] == position[None, :]
    pick = hit.astype(BF)
    slot_row = jnp.sum(jnp.where(hit, token_row[None, :] + 1, 0), axis=1) - 1
    token_weight = combine_weight[:, 0]
    scaled_grad = (token_weight[:, None] * cotangent.astype(F32)).astype(BF)
    sent = dot(pick, scaled_grad).astype(BF).reshape(experts, capacity, width)
    grad_rows = lax.all_to_all(sent, "expert", split_axis=0, concat_axis=0, tiled=True)
    grad_rows = grad_rows.reshape(-1, width)
    rows = lax.all_to_all(
        slot_row.reshape(experts, capacity), "expert", split_axis=0, concat_axis=0, tiled=True
    ).reshape(-1)
    select = (rows[:, None] == jnp.arange(table_rows, dtype=jnp.int32)[None, :]).astype(BF)
    gate_act = dot(table, gate_weight[0])
    up_act = dot(table, up_weight[0])
    half = (jax.nn.silu(gate_act) * up_act).astype(BF)
    hidden = lax.all_gather(half, "dp", axis=1, tiled=True)
    out_rows = dot(hidden, down_weight[0]).astype(BF)
    sent_out = dot(select, out_rows).astype(BF).reshape(-1, capacity, width)
    hidden_rows = dot(select, hidden).astype(BF)
    down_grad = dot(hidden_rows, grad_rows, ((0,), (0,))).astype(BF)
    returned = lax.all_to_all(sent_out, "expert", split_axis=0, concat_axis=0, tiled=True)
    token_out = dot(pick, returned.reshape(experts * capacity, width), ((0,), (0,)))
    mixed = (token_weight[:, None] * token_out).astype(BF)
    return (mixed, down_grad[None])


def solution(mesh):
    return jax.shard_map(
        body,
        mesh=mesh,
        in_specs=(
            P("dp", None, None),
            P(None, "expert", None),
            P("expert", None),
            P("expert", None),
            P("expert", "dp"),
            P(),
            P("expert", None, "dp"),
            P("expert", None, "dp"),
            P("expert", None, "dp"),
            P("expert", "dp"),
        ),
        out_specs=(P("expert", "dp"), P("expert", None, "dp")),
        check_vma=False,
    )
```

profile of v0, /device:TPU:9, one launch (start us, length us, event | category | flops | bytes accessed | tf_op | source)
XLA Modules:
  0.0 144.0 jit_solution(15097482984221297119)
XLA Ops:
  7.2 1.9 %copy.17 = bf16[72,1024]{0,1:T(8,128)(2,1)} copy(bf16[72,1024]{1,0:T(8,128)(2,1)} %param.14) | data formatting | bytes 294912 | tf_op jit(solution)/shard_map/reshape | solution.py:33
  9.1 6.6 %all-to-all-start.1 = ((bf16[72,16,64]{0,2,1:T(8,128)(2,1)}), bf16[72,16,64]{0,2,1:T(8,128)(2,1)}, u32[]{:S(2)}, u32[]{:S(2)}) async-start(bf16[72,16,64]{0,2,1:T(8,128)(2,1)} %bitcast.3), calls=%async_computation.1 | async-start | bytes 524288 | tf_op jit(solution)/shard_map/all_to_all | solution.py:32
  15.7 9.1 %all_gather.9 = bf16[4,64,1152]{2,1,0:T(8,128)(2,1)S(1)} all-gather(bf16[2,64,1152]{2,1,0:T(8,128)(2,1)} %param.10), channel_id=1, replica_groups=mesh['dp'=2,'expert'=16] {'dp'}, dimensions={0}, use_global_device_ids=true | all-gather | bytes 884736 | tf_op jit(solution)/shard_map/all_gather | solution.py:30
  24.9 1.8 %copy.16 = bf16[16,72,1,64]{1,0,3,2:T(8,128)(2,1)} copy(bf16[16,72,1,64]{1,3,0,2:T(8,128)(2,1)} %bitcast.5) | data formatting | bytes 294912 | tf_op jit(solution)/shard_map/all_to_all | solution.py:32
  26.7 1.9 %reshape.87 = bf16[1152,64]{0,1:T(8,128)(2,1)} reshape(bf16[16,72,1,64]{1,0,3,2:T(8,128)(2,1)} %copy.16) | data formatting | bytes 294912 | tf_op jit(solution)/shard_map/reshape | solution.py:34
  28.6 1.8 %convolution_convert_fusion.4 = bf16[256,64]{0,1:T(8,128)(2,1)} fusion(bf16[256,1152]{1,0:T(8,128)(2,1)S(1)} %bitcast.36, bf16[1152,64]{0,1:T(8,128)(2,1)} %reshape.87), kind=kOutput, calls=%fused_computation.21 | convolution fusion | flops 37765120 | bytes 770048 | tf_op jit(solution)/shard_map/dot_general | solution.py:11
  31.8 6.8 %all-to-all-start = ((s32[16,1,20]{2,1,0:T(1,128)}), s32[16,1,20]{2,1,0:T(1,128)S(1)}, u32[]{:S(2)}, u32[]{:S(2)}) async-start(s32[16,1,20]{2,1,0:T(1,128)} %sub.7), calls=%async_computation | async-start | bytes 16384 | tf_op jit(solution)/shard_map/all_to_all | solution.py:59
  38.6 1.5 %convolution_convert_fusion.2 = bf16[320,1024]{1,0:T(8,128)(2,1)S(1)} fusion(bf16[256,1024]{1,0:T(8,128)(2,1)} %param.19, f32[256]{0:T(256)S(1)} %bitcast.39, s32[256]{0:T(256)S(1)} %multiply_add_fusion), kind=kOutput, calls=%fused_computation.15 | convolution fusion | flops 168968192 | bytes 1181696 | tf_op jit(solution)/shard_map/dot_general | solution.py:11
  40.1 1.0 reshape.90
  41.1 2.2 %all-to-all-done = s32[16,1,20]{2,1,0:T(1,128)S(1)} async-done(((s32[16,1,20]{2,1,0:T(1,128)}), s32[16,1,20]{2,1,0:T(1,128)S(1)}, u32[]{:S(2)}, u32[]{:S(2)}) %all-to-all-start) | async-done | bytes 1312 | tf_op jit(solution)/shard_map/all_to_all | solution.py:59
  43.3 5.8 %all-to-all-start.3 = ((bf16[16,20,1024]{2,1,0:T(8,128)(2,1)}), bf16[16,20,1024]{2,1,0:T(8,128)(2,1)}, u32[]{:S(2)}, u32[]{:S(2)}) async-start(bf16[16,20,1024]{2,1,0:T(8,128)(2,1)} %reshape.90), calls=%async_computation.3 | async-start | bytes 1572864 | tf_op jit(solution)/shard_map/all_to_all | solution.py:57
  50.5 38.2 %all-gather.2.cloned.1.call-done = bf16[256,2048]{0,1:T(8,128)(2,1)} async-done(((bf16[256,64]{0,1:T(8,128)(2,1)}), bf16[256,2048]{0,1:T(8,128)(2,1)}) %all-gather.2.cloned.1.call-update) | async-done | bytes 1048592 | tf_op jit(solution)/shard_map/all_gather | solution.py:36
  88.7 1.5 %fusion.7 = f32[256]{0:T(256)S(1)} fusion(bf16[256,2048]{0,1:T(8,128)(2,1)} %all-gather.2.cloned.1.call-done), kind=kLoop, calls=%fused_computation.11 | loop fusion | flops 1572608 | bytes 1049600 | tf_op jit(solution)/shard_map/reduce_sum | solution.py:38
  90.3 3.3 %fusion.5 = f32[256,704]{0,1:T(8,128)S(1)} fusion(bf16[1,2048,704]{1,2,0:T(8,128)(2,1)} %param.16, bf16[256,2048]{0,1:T(8,128)(2,1)} %all-gather.2.cloned.1.call-done, f32[2048]{0:T(1024)} %param.15, f32[256]{0:T(256)S(1)} %add_rsqrt_fusion), kind=kOutput, calls=%fused_computation.6 | convolution fusion | flops 740294656 | bytes 4662272 | tf_op jit(solution)/shard_map/dot_general | solution.py:11
  93.7 1.0 fusion.17
  94.7 10.6 %all_gather.11 = bf16[256,1408]{0,1:T(8,128)(2,1)} all-gather(bf16[256,704]{0,1:T(8,128)(2,1)S(1)} %fusion.17), channel_id=1, replica_groups=mesh['dp'=2,'expert'=16] {'dp'}, dimensions={1}, use_global_device_ids=true | all-gather | bytes 1081344 | tf_op jit(solution)/shard_map/all_gather | solution.py:66
  105.3 2.3 %convolution_convert_fusion.3 = bf16[320,1024]{1,0:T(8,128)(2,1)S(1)} fusion(bf16[256,1408]{0,1:T(8,128)(2,1)} %all_gather.11, bf16[1,1408,1024]{2,1,0:T(8,128)(2,1)S(1)} %copy-done, s32[320]{0:T(512)S(1)} %eq.47), kind=kOutput, calls=%fused_computation.16 | convolution fusion | flops 906641408 | bytes 4261120 | tf_op jit(solution)/shard_map/dot_general | solution.py:11
  107.6 1.0 reshape.88
  108.7 6.3 %all-to-all-start.2 = ((bf16[16,20,1024]{2,1,0:T(8,128)(2,1)}), bf16[16,20,1024]{2,1,0:T(8,128)(2,1)}, u32[]{:S(2)}, u32[]{:S(2)}) async-start(bf16[16,20,1024]{2,1,0:T(8,128)(2,1)} %reshape.88), calls=%async_computation.2 | async-start | bytes 1572864 | tf_op jit(solution)/shard_map/all_to_all | solution.py:71
  114.9 1.2 reshape.91
  116.2 4.7 %fusion = bf16[1,1408,1024]{2,1,0:T(8,128)(2,1)} fusion(bf16[320,1024]{1,0:T(8,128)(2,1)S(1)} %reshape.91, bf16[256,1408]{0,1:T(8,128)(2,1)} %all_gather.11, s32[320]{0:T(512)S(1)} %eq.47), kind=kOutput, calls=%fused_computation.1 | convolution fusion | flops 1155407872 | bytes 4261120 | tf_op jit(solution)/shard_map/dot_general | solution.py:11
  120.8 13.7 %all-to-all-done.2 = bf16[16,20,1024]{2,1,0:T(8,128)(2,1)} async-done(((bf16[16,20,1024]{2,1,0:T(8,128)(2,1)}), bf16[16,20,1024]{2,1,0:T(8,128)(2,1)}, u32[]{:S(2)}, u32[]{:S(2)}) %all-to-all-start.2) | async-done | bytes 655392 | tf_op jit(solution)/shard_map/all_to_all | solution.py:71
  134.6 1.2 reshape.89
  135.8 1.3 fusion.13
  (31 shorter events, 2.8 us)
Async XLA Ops:
  7.2 98.1 %copy-start = (bf16[1,1408,1024]{2,1,0:T(8,128)(2,1)S(1)}, bf16[1,1408,1024]{2,1,0:T(8,128)(2,1)}, u32[]{:S(2)}) copy-start(bf16[1,1408,1024]{2,1,0:T(8,128)(2,1)} %param.18) | copy-start | bytes 8650756
  7.2 23.3 %copy-start.4 = (s32[2,1,2]{2,1,0:T(1,128)S(1)}, s32[2,1,2]{2,1,0:T(1,128)}, u32[]{:S(2)}) copy-start(s32[2,1,2]{2,1,0:T(1,128)} %param.11) | copy-start | bytes 52
  7.2 23.5 %copy-start.2 = (s32[256,1]{0,1:T(1,128)S(1)}, s32[256,1]{0,1:T(1,128)}, u32[]{:S(2)}) copy-start(s32[256,1]{0,1:T(1,128)} %param.12) | copy-start | bytes 3076
  7.2 31.4 %copy-start.3 = (f32[256,1]{0,1:T(1,128)S(1)}, f32[256,1]{0,1:T(1,128)}, u32[]{:S(2)}) copy-start(f32[256,1]{0,1:T(1,128)} %param.13) | copy-start | bytes 3076
  9.1 15.8 %all-to-all-start.1 = ((bf16[72,16,64]{0,2,1:T(8,128)(2,1)}), bf16[72,16,64]{0,2,1:T(8,128)(2,1)}, u32[]{:S(2)}, u32[]{:S(2)}) async-start(bf16[72,16,64]{0,2,1:T(8,128)(2,1)} %bitcast.3), calls=%async_computation.1 | async-start | bytes 524288 | tf_op jit(solution)/shard_map/all_to_all | solution.py:32
  15.7 73.1 %all-gather.2.cloned.1.call-start = ((), (), s32[]{:S(2)}) async-start(), calls=%async_computation.4 | async-start | bytes 1081344 | tf_op jit(solution)/shard_map/all_gather | solution.py:36
  31.8 11.5 %all-to-all-start = ((s32[16,1,20]{2,1,0:T(1,128)}), s32[16,1,20]{2,1,0:T(1,128)S(1)}, u32[]{:S(2)}, u32[]{:S(2)}) async-start(s32[16,1,20]{2,1,0:T(1,128)} %sub.7), calls=%async_computation | async-start | bytes 16384 | tf_op jit(solution)/shard_map/all_to_all | solution.py:59
  43.3 65.3 %all-to-all-start.3 = ((bf16[16,20,1024]{2,1,0:T(8,128)(2,1)}), bf16[16,20,1024]{2,1,0:T(8,128)(2,1)}, u32[]{:S(2)}, u32[]{:S(2)}) async-start(bf16[16,20,1024]{2,1,0:T(8,128)(2,1)} %reshape.90), calls=%async_computation.3 | async-start | bytes 1572864 | tf_op jit(solution)/shard_map/all_to_all | solution.py:57
  90.3 3.3 %copy-start.1 = (bf16[256,2048]{0,1:T(8,128)(2,1)S(1)}, bf16[256,2048]{0,1:T(8,128)(2,1)}, u32[]{:S(2)}) copy-start(bf16[256,2048]{0,1:T(8,128)(2,1)} %all-gather.2.cloned.1.call-done) | copy-start | bytes 3145732
  90.3 3.3 %copy-start.5 = (bf16[1,2048,704]{1,2,0:T(8,128)(2,1)S(1)}, bf16[1,2048,704]{1,2,0:T(8,128)(2,1)}, u32[]{:S(2)}) copy-start(bf16[1,2048,704]{1,2,0:T(8,128)(2,1)} %param.17) | copy-start | bytes 8650756
  90.3 3.3 %copy-start.6 = (f32[2048]{0:T(1024)S(1)}, f32[2048]{0:T(1024)}, u32[]{:S(2)}) copy-start(f32[2048]{0:T(1024)} %param.15) | copy-start | bytes 24580
  108.7 25.9 %all-to-all-start.2 = ((bf16[16,20,1024]{2,1,0:T(8,128)(2,1)}), bf16[16,20,1024]{2,1,0:T(8,128)(2,1)}, u32[]{:S(2)}, u32[]{:S(2)}) async-start(bf16[16,20,1024]{2,1,0:T(8,128)(2,1)} %reshape.88), calls=%async_computation.2 | async-start | bytes 1572864 | tf_op jit(solution)/shard_map/all_to_all | solution.py:71
Sparse Core Ops, SparseCore 0:
  30.6 58.1 all-gather.1
where the time goes:
time: 145 us; the launch traced here: 144 us
  waiting for transfers between devices  54.2 us (37%)
  starting transfers between devices  25.6 us (18%)
  blocking collectives  19.7 us (14%)
  matrix products  16 us (11%)
  between operations  14.2 us (10%)
  local copies, waits for them, and re-layouts  11.7 us (8%)
  other arithmetic  2.68 us (2%)
    all_gather x1, waiting for transfers between devices, body(): projected = lax.all_gather(part, ('dp', 'expert'), axis=1, tiled=True)  38.2 us
    dot_general x7, matrix products, dot(): return lax.dot_general(a, b, (dims, ((), ())), preferred_element_type=F32)  16 us
    all_to_all x1, waiting for transfers between devices, body(): lax.all_to_all(sent_out, 'expert', split_axis=0, concat_axis=0, tiled=True)  13.7 us
    all_gather x1, blocking collectives, body(): hidden = lax.all_gather(half, 'dp', axis=1, tiled=True)  10.6 us
    all_gather x1, blocking collectives, body(): feats = lax.all_gather(cache, 'dp', axis=0, tiled=True).reshape(-1, feat)  9.12 us
    all_to_all x1, starting transfers between devices, body(): lax.all_to_all(slot_row.reshape(experts, capacity), 'expert', split_axis=...  6.85 us
    all_to_all x1, starting transfers between devices, body(): lax.all_to_all(proj_weight.reshape(-1, n_expert, lanes), 'expert', split_...  6.58 us
    all_to_all x1, starting transfers between devices, body(): lax.all_to_all(sent_out, 'expert', split_axis=0, concat_axis=0, tiled=True)  6.26 us
  transfers between devices with their start and end apart: 5, of which 3 were waited for; matrix products, arithmetic and copies ran while one was open for 14% of the time, Pallas kernels for 0%

commit v1 on v0

--- a/solution.py
+++ b/solution.py
@@ -5,6 +5,18 @@
 
 BF = jnp.bfloat16
 F32 = jnp.float32
+
+
+def report_space_up(inner_x):
+    return jnp.concatenate(
+        jax.lax.all_to_all(
+            jnp.stack(jnp.split(inner_x, jax.lax.axis_size("expert"), axis=1)),
+            axis_name="expert",
+            split_axis=0,
+            concat_axis=0,
+        ),
+        axis=0,
+    )
 
 
 def dot(a, b, dims=((1,), (0,))):
@@ -29,9 +41,7 @@
     block, feat = cache.shape[1:]
     feats = lax.all_gather(cache, "dp", axis=0, tiled=True).reshape(-1, feat)
     lanes = width // n_expert
-    piece = lax.all_to_all(
-        proj_weight.reshape(-1, n_expert, lanes), "expert", split_axis=1, concat_axis=0, tiled=True
-    ).reshape(feat, lanes)
+    piece = report_space_up(proj_weight.reshape(-1, n_expert, lanes)).reshape(feat, lanes)
     part = dot(feats, piece).astype(BF)
     projected = lax.all_gather(part, ("dp", "expert"), axis=1, tiled=True)
     values = projected.astype(F32)

time: 145 us -> 162 us (1.12)
  local copies, waits for them, and re-layouts: 11.7 us -> 28.1 us
    unnamed x14 -> x29, local copies, waits for them, and re-layouts: 0.04 us -> 9.17 us
    split x0 -> x17, local copies, waits for them, and re-layouts: none -> 7.31 us  [report_space_up(): jnp.split(inner_x, jax.lax.axis_size('expert'), axis=1)]
    another operation x0 -> x2, local copies, waits for them, and re-layouts: none -> 2.5 us  [the longest x1 1.89 us: body(): report_space_up(proj_weight.reshape(-1, n_expert, lanes))]
    reshape x1 -> x0, local copies, waits for them, and re-layouts: 1.89 us -> none  [body(): piece = lax.all_to_all(proj_weight.reshape(-1, n_expert, lanes), 'expert'...]
  transfers between devices with their start and end apart: 5 -> 5, of which waited for: 3 -> 3; matrix products, arithmetic and copies ran while one was open for 14% -> 13% of each run, Pallas kernels for 0% -> 0%
where the time goes in v1:
time: 162 us; the launch traced here: 161 us
  waiting for transfers between devices  54.4 us (34%)
  local copies, waits for them, and re-layouts  28.1 us (17%)
  starting transfers between devices  25.6 us (16%)
  blocking collectives  19.7 us (12%)
  matrix products  16 us (10%)
  between operations  14.3 us (9%)
  other arithmetic  2.54 us (2%)
    all_gather x1, waiting for transfers between devices, body(): projected = lax.all_gather(part, ('dp', 'expert'), axis=1, tiled=True)  38.5 us
    dot_general x7, matrix products, dot(): return lax.dot_general(a, b, (dims, ((), ())), preferred_element_type=F32)  16 us
    all_to_all x1, waiting for transfers between devices, body(): lax.all_to_all(sent_out, 'expert', split_axis=0, concat_axis=0, tiled=True)  13.7 us
    all_gather x1, blocking collectives, body(): hidden = lax.all_gather(half, 'dp', axis=1, tiled=True)  10.6 us
    unnamed x29, local copies, waits for them, and re-layouts  9.17 us
    all_gather x1, blocking collectives, body(): feats = lax.all_gather(cache, 'dp', axis=0, tiled=True).reshape(-1, feat)  9.12 us
    split x17, local copies, waits for them, and re-layouts, report_space_up(): jnp.split(inner_x, jax.lax.axis_size('expert'), axis=1)  7.31 us
    all_to_all x1, starting transfers between devices, body(): lax.all_to_all(slot_row.reshape(experts, capacity), 'expert', split_axis=...  6.85 us
  transfers between devices with their start and end apart: 5, of which 3 were waited for; matrix products, arithmetic and copies ran while one was open for 13% of the time, Pallas kernels for 0%

profile of v1, /device:TPU:9, one launch (start us, length us, event | category | flops | bytes accessed | tf_op | source)
XLA Modules:
  0.0 160.5 jit_solution(14853586819270656399)
XLA Ops:
  7.2 1.3 reshape.81
  8.5 1.1 fusion.32
  25.6 6.6 %all-to-all-start.1 = ((bf16[16,72,1,64]{1,3,2,0:T(8,128)(2,1)}), bf16[16,72,1,64]{1,3,2,0:T(8,128)(2,1)}, u32[]{:S(2)}, u32[]{:S(2)}) async-start(bf16[16,72,1,64]{1,3,2,0:T(8,128)(2,1)} %constant_dynamic-update-slice_fusion), calls=%async_computation.1 | async-start | bytes 524288 | tf_op jit(solution)/shard_map/all_to_all | solution.py:12
  32.3 9.1 %all_gather.9 = bf16[4,64,1152]{2,1,0:T(8,128)(2,1)S(1)} all-gather(bf16[2,64,1152]{2,1,0:T(8,128)(2,1)} %param.10), channel_id=1, replica_groups=mesh['dp'=2,'expert'=16] {'dp'}, dimensions={0}, use_global_device_ids=true | all-gather | bytes 884736 | tf_op jit(solution)/shard_map/all_gather | solution.py:42
  41.4 1.8 %copy.438 = bf16[16,72,1,64]{1,0,3,2:T(8,128)(2,1)} copy(bf16[16,72,1,64]{1,3,2,0:T(8,128)(2,1)} %all-to-all-done.1) | data formatting | bytes 294912 | tf_op jit(solution)/shard_map/all_to_all | solution.py:12
  43.2 1.9 %reshape_reshape.3 = bf16[1152,64]{0,1:T(8,128)(2,1)} reshape(bf16[16,72,1,64]{1,0,3,2:T(8,128)(2,1)} %copy.438) | data formatting | bytes 294912 | tf_op jit(solution)/shard_map/reshape;reshape | solution.py:44
  45.1 1.8 %fusion.22 = bf16[256,64]{0,1:T(8,128)(2,1)} fusion(bf16[1152,64]{0,1:T(8,128)(2,1)} %reshape_reshape.3, bf16[256,1152]{1,0:T(8,128)(2,1)S(1)} %bitcast.66), kind=kOutput, calls=%fused_computation.22 | convolution fusion | flops 37765120 | bytes 770048 | tf_op jit(solution)/shard_map/dot_general | solution.py:23
  48.3 6.8 %all-to-all-start = ((s32[16,1,20]{2,1,0:T(1,128)}), s32[16,1,20]{2,1,0:T(1,128)S(1)}, u32[]{:S(2)}, u32[]{:S(2)}) async-start(s32[16,1,20]{2,1,0:T(1,128)} %sub.7), calls=%async_computation | async-start | bytes 16384 | tf_op jit(solution)/shard_map/all_to_all | solution.py:69
  55.1 1.5 convolution_convert_fusion.2
  57.6 2.2 %all-to-all-done = s32[16,1,20]{2,1,0:T(1,128)S(1)} async-done(((s32[16,1,20]{2,1,0:T(1,128)}), s32[16,1,20]{2,1,0:T(1,128)S(1)}, u32[]{:S(2)}, u32[]{:S(2)}) %all-to-all-start) | async-done | bytes 1312 | tf_op jit(solution)/shard_map/all_to_all | solution.py:69
  59.8 5.8 %all-to-all-start.3 = ((bf16[16,20,1024]{2,1,0:T(8,128)(2,1)}), bf16[16,20,1024]{2,1,0:T(8,128)(2,1)}, u32[]{:S(2)}, u32[]{:S(2)}) async-start(bf16[16,20,1024]{2,1,0:T(8,128)(2,1)} %reshape.85), calls=%async_computation.3 | async-start | bytes 1572864 | tf_op jit(solution)/shard_map/all_to_all | solution.py:67
  66.8 38.5 %all-gather.2.cloned.1.call-done = bf16[256,2048]{0,1:T(8,128)(2,1)} async-done(((bf16[256,64]{0,1:T(8,128)(2,1)}), bf16[256,2048]{0,1:T(8,128)(2,1)}) %all-gather.2.cloned.1.call-update) | async-done | bytes 1048592 | tf_op jit(solution)/shard_map/all_gather | solution.py:46
  105.3 1.5 fusion.7
  106.8 3.3 %fusion.5 = f32[256,704]{0,1:T(8,128)S(1)} fusion(bf16[1,2048,704]{1,2,0:T(8,128)(2,1)} %param.16, bf16[256,2048]{0,1:T(8,128)(2,1)} %all-gather.2.cloned.1.call-done, f32[2048]{0:T(1024)} %param.15, f32[256]{0:T(256)S(1)} %add_rsqrt_fusion), kind=kOutput, calls=%fused_computation.6 | convolution fusion | flops 740294656 | bytes 4662272 | tf_op jit(solution)/shard_map/dot_general | solution.py:23
  110.2 1.0 fusion.17
  111.2 10.6 %all_gather.11 = bf16[256,1408]{0,1:T(8,128)(2,1)} all-gather(bf16[256,704]{0,1:T(8,128)(2,1)S(1)} %fusion.17), channel_id=1, replica_groups=mesh['dp'=2,'expert'=16] {'dp'}, dimensions={1}, use_global_device_ids=true | all-gather | bytes 1081344 | tf_op jit(solution)/shard_map/all_gather | solution.py:76
  121.8 2.3 %convolution_convert_fusion.3 = bf16[320,1024]{1,0:T(8,128)(2,1)S(1)} fusion(bf16[256,1408]{0,1:T(8,128)(2,1)} %all_gather.11, bf16[1,1408,1024]{2,1,0:T(8,128)(2,1)S(1)} %copy-done, s32[320]{0:T(512)S(1)} %eq.47), kind=kOutput, calls=%fused_computation.16 | convolution fusion | flops 906641408 | bytes 4261120 | tf_op jit(solution)/shard_map/dot_general | solution.py:23
  124.1 1.0 reshape.83
  125.2 6.3 %all-to-all-start.2 = ((bf16[16,20,1024]{2,1,0:T(8,128)(2,1)}), bf16[16,20,1024]{2,1,0:T(8,128)(2,1)}, u32[]{:S(2)}, u32[]{:S(2)}) async-start(bf16[16,20,1024]{2,1,0:T(8,128)(2,1)} %reshape.83), calls=%async_computation.2 | async-start | bytes 1572864 | tf_op jit(solution)/shard_map/all_to_all | solution.py:81
  131.5 1.2 reshape.86
  132.7 4.7 %fusion = bf16[1,1408,1024]{2,1,0:T(8,128)(2,1)} fusion(bf16[320,1024]{1,0:T(8,128)(2,1)S(1)} %reshape.86, bf16[256,1408]{0,1:T(8,128)(2,1)} %all_gather.11, s32[320]{0:T(512)S(1)} %eq.47), kind=kOutput, calls=%fused_computation.1 | convolution fusion | flops 1155407872 | bytes 4261120 | tf_op jit(solution)/shard_map/dot_general | solution.py:23
  137.4 13.7 %all-to-all-done.2 = bf16[16,20,1024]{2,1,0:T(8,128)(2,1)} async-done(((bf16[16,20,1024]{2,1,0:T(8,128)(2,1)}), bf16[16,20,1024]{2,1,0:T(8,128)(2,1)}, u32[]{:S(2)}, u32[]{:S(2)}) %all-to-all-start.2) | async-done | bytes 655392 | tf_op jit(solution)/shard_map/all_to_all | solution.py:81
  151.1 1.2 reshape.84
  152.4 1.3 fusion.13
  (64 shorter events, 19.5 us)
Async XLA Ops:
  7.2 114.6 %copy-start = (bf16[1,1408,1024]{2,1,0:T(8,128)(2,1)S(1)}, bf16[1,1408,1024]{2,1,0:T(8,128)(2,1)}, u32[]{:S(2)}) copy-start(bf16[1,1408,1024]{2,1,0:T(8,128)(2,1)} %param.18) | copy-start | bytes 8650756
  8.5 38.5 %copy-start.4 = (s32[2,1,2]{2,1,0:T(1,128)S(1)}, s32[2,1,2]{2,1,0:T(1,128)}, u32[]{:S(2)}) copy-start(s32[2,1,2]{2,1,0:T(1,128)} %param.11) | copy-start | bytes 52
  8.5 38.8 %copy-start.2 = (s32[256,1]{0,1:T(1,128)S(1)}, s32[256,1]{0,1:T(1,128)}, u32[]{:S(2)}) copy-start(s32[256,1]{0,1:T(1,128)} %param.12) | copy-start | bytes 3076
  25.6 15.8 %all-to-all-start.1 = ((bf16[16,72,1,64]{1,3,2,0:T(8,128)(2,1)}), bf16[16,72,1,64]{1,3,2,0:T(8,128)(2,1)}, u32[]{:S(2)}, u32[]{:S(2)}) async-start(bf16[16,72,1,64]{1,3,2,0:T(8,128)(2,1)} %constant_dynamic-update-slice_fusion), calls=%async_computation.1 | async-start | bytes 524288 | tf_op jit(solution)/shard_map/all_to_all | solution.py:12
  32.2 73.1 %all-gather.2.cloned.1.call-start = ((), (), s32[]{:S(2)}) async-start(), calls=%async_computation.4 | async-start | bytes 1081344 | tf_op jit(solution)/shard_map/all_gather | solution.py:46
  48.3 11.5 %all-to-all-start = ((s32[16,1,20]{2,1,0:T(1,128)}), s32[16,1,20]{2,1,0:T(1,128)S(1)}, u32[]{:S(2)}, u32[]{:S(2)}) async-start(s32[16,1,20]{2,1,0:T(1,128)} %sub.7), calls=%async_computation | async-start | bytes 16384 | tf_op jit(solution)/shard_map/all_to_all | solution.py:69
  59.8 65.3 %all-to-all-start.3 = ((bf16[16,20,1024]{2,1,0:T(8,128)(2,1)}), bf16[16,20,1024]{2,1,0:T(8,128)(2,1)}, u32[]{:S(2)}, u32[]{:S(2)}) async-start(bf16[16,20,1024]{2,1,0:T(8,128)(2,1)} %reshape.85), calls=%async_computation.3 | async-start | bytes 1572864 | tf_op jit(solution)/shard_map/all_to_all | solution.py:67
  106.8 3.3 %copy-start.1 = (bf16[256,2048]{0,1:T(8,128)(2,1)S(1)}, bf16[256,2048]{0,1:T(8,128)(2,1)}, u32[]{:S(2)}) copy-start(bf16[256,2048]{0,1:T(8,128)(2,1)} %all-gather.2.cloned.1.call-done) | copy-start | bytes 3145732
  106.8 3.3 %copy-start.5 = (bf16[1,2048,704]{1,2,0:T(8,128)(2,1)S(1)}, bf16[1,2048,704]{1,2,0:T(8,128)(2,1)}, u32[]{:S(2)}) copy-start(bf16[1,2048,704]{1,2,0:T(8,128)(2,1)} %param.17) | copy-start | bytes 8650756
  106.8 3.3 %copy-start.6 = (f32[2048]{0:T(1024)S(1)}, f32[2048]{0:T(1024)}, u32[]{:S(2)}) copy-start(f32[2048]{0:T(1024)} %param.15) | copy-start | bytes 24580
  125.2 25.9 %all-to-all-start.2 = ((bf16[16,20,1024]{2,1,0:T(8,128)(2,1)}), bf16[16,20,1024]{2,1,0:T(8,128)(2,1)}, u32[]{:S(2)}, u32[]{:S(2)}) async-start(bf16[16,20,1024]{2,1,0:T(8,128)(2,1)} %reshape.83), calls=%async_computation.2 | async-start | bytes 1572864 | tf_op jit(solution)/shard_map/all_to_all | solution.py:81
  132.7 19.7 %copy-start.3 = (f32[256,1]{0,1:T(1,128)S(1)}, f32[256,1]{0,1:T(1,128)}, u32[]{:S(2)}) copy-start(f32[256,1]{0,1:T(1,128)} %param.13) | copy-start | bytes 3076
Sparse Core Ops, SparseCore 0:
  47.1 58.1 all-gather.1
